TPU v7x, 512 devices: a whole 4x4x16 slice. The times are simulated.
512 devices in a mesh: rep: 32 (over y_hi, z), fsdp: 16 (over y_lo, x, core).
Axes of the slice: x: 4, y: 4 (y_hi: 2, y_lo: 2; y = y_hi * 2 + y_lo), z: 16, core: 2. Of those that a mesh axis runs over, the one named last changes fastest.
Arguments:
- codes: int32 [32, 2, 32, 28672], P('rep', None, 'fsdp'), may hold values from -127 to 127
- scales: float32 [32, 2, 32], P('rep', None, 'fsdp'), may hold values from 0.004 to 0.04
- outer_params: float32 [2, 32, 28672], P(None, 'fsdp', 'rep'), may hold values from -6 to 6
- momentum: float32 [2, 32, 28672], P(None, 'fsdp', 'rep'), may hold values from -4 to 4
- local_params: bfloat16 [32, 2, 32, 28672], P('rep', None, 'fsdp'), may hold values from -6 to 6
- rates: float32 [32], replicated, may hold values from 0.35 to 1.4
- slot: int32 [32], replicated, may hold values from 0 to 31, each once
- tokens: bfloat16 [65536, 7168], P(('rep', 'fsdp')), may hold values from -6 to 6
- gain: bfloat16 [32, 7168], P('rep', 'fsdp'), may hold values from 0.5 to 1.5
- kv_weight: bfloat16 [32, 7168, 1024], P('rep', 'fsdp'), may hold values from -0.0625 to 0.0625
Outputs:
- keyvals: bfloat16 [65536, 1024], P(('rep', 'fsdp'))
- new_outer: float32 [2, 32, 28672], P(None, 'fsdp', 'rep')
- new_momentum: float32 [2, 32, 28672], P(None, 'fsdp', 'rep')
- blended: bfloat16 [32, 2, 32, 28672], P('rep', None, 'fsdp')
Inputs may be any that keep to these rules, and one draw needn't show every extreme that they name: slot holds each of 0 to 31 once.
All inputs are finite; a program needn't handle non-finite values.
Results may differ from a plain program's by a relative error of at most 0.005.
Values may be sent and summed in bfloat16 or wider, within the bound.
A program may use at most 128 MiB of HBM per device.

v0:
```python
import jax
import jax.numpy as jnp
from jax import lax
from jax.sharding import PartitionSpec as P


def inner_step(tokens, gain, kv_weight):
    values = tokens.astype(jnp.float32)
    inverse = lax.rsqrt(jnp.mean(values * values, axis=1, keepdims=True) + 1e-05)
    scaled = values * inverse
    weight_piece = lax.all_gather(kv_weight, "fsdp", axis=1, tiled=True)
    gain_piece = lax.all_gather(gain, "fsdp", axis=1, tiled=True)
    normed = (scaled * gain_piece[0].astype(jnp.float32)).astype(jnp.bfloat16)
    total = jnp.dot(normed, weight_piece[0], preferred_element_type=jnp.float32)
    return total.astype(jnp.bfloat16)


def outer_step(codes, scales, outer_params, momentum, local_params, rates, slot):
    replicas = lax.axis_size("rep")
    term = codes[0].astype(jnp.float32) * scales[0][..., None]
    positions = jnp.arange(rates.shape[0], dtype=jnp.int32)
    rate = jnp.sum(jnp.where(positions == slot[0], rates, 0.0))
    summed = lax.psum(term, "rep")
    mean_delta = summed / replicas
    params_full, moment_full = (
        lax.all_gather(outer_params, "rep", axis=2, tiled=True),
        lax.all_gather(momentum, "rep", axis=2, tiled=True),
    )
    moment_next = 0.9 * moment_full + mean_delta
    params_next = params_full - rate * (mean_delta + 0.9 * moment_next)
    width = outer_params.shape[2]
    offset = lax.axis_index("rep") * width
    new_momentum = lax.dynamic_slice_in_dim(moment_next, offset, width, 2)
    new_outer = lax.dynamic_slice_in_dim(params_next, offset, width, 2)
    blended = (0.5 * local_params.astype(jnp.float32) + 0.5 * params_next[None]).astype(
        jnp.bfloat16
    )
    return (new_outer, new_momentum, blended)


def shards(
    codes, scales, outer_params, momentum, local_params, rates, slot, tokens, gain, kv_weight
):
    new_outer, new_momentum, blended = outer_step(
        codes, scales, outer_params, momentum, local_params, rates, slot
    )
    keyvals = inner_step(tokens, gain, kv_weight)
    return (keyvals, new_outer, new_momentum, blended)


def solution(mesh):
    return jax.shard_map(
        shards,
        mesh=mesh,
        in_specs=(
            P("rep", None, "fsdp", None),
            P("rep", None, "fsdp"),
            P(None, "fsdp", "rep"),
            P(None, "fsdp", "rep"),
            P("rep", None, "fsdp", None),
            P(),
            P(),
            P(("rep", "fsdp"), None),
            P("rep", "fsdp"),
            P("rep", "fsdp", None),
        ),
        out_specs=(
            P(("rep", "fsdp"), None),
            P(None, "fsdp", "rep"),
            P(None, "fsdp", "rep"),
            P("rep", None, "fsdp", None),
        ),
        check_vma=False,
    )
```

profile of v0, /device:TPU:24, one launch (start us, length us, event | category | flops | bytes accessed | tf_op | source)
XLA Modules:
  0.0 330.5 jit_solution(12225780211498964110)
XLA Ops:
  8.0 0.0 copy-start
  8.0 0.0 copy-start.1
  8.0 0.0 all-reduce.3.cloned.1.call-start
  8.1 2.1 bitcast_multiply_fusion
  10.2 0.0 all-reduce.3.cloned.1.call-update
  10.2 0.0 all-gather.2.cloned.1.call-start
  10.3 0.5 all-gather.2.cloned.1.call-update
  10.8 0.7 reduce
  11.5 1.3 dynamic-slice
  13.5 0.3 dynamic-update-slice
  13.7 56.3 %all-reduce = bf16[7168]{0:T(1024)(128)(2,1)S(1)} all-reduce(bf16[7168]{0:T(1024)(128)(2,1)S(1)} %dynamic-update-slice), channel_id=1, replica_groups=mesh['rep'=32,'fsdp'=16] {'fsdp'}, use_global_device_ids=true, to_apply=%add | all-reduce | flops 7168 | bytes 28672
  70.0 1.9 fusion.15
  71.9 84.0 %all_gather.14 = f32[2,2,28672]{2,1,0:T(2,128)S(1)} all-gather(f32[2,2,896]{2,1,0:T(2,128)} %param.12), channel_id=1, replica_groups=mesh['rep'=32,'fsdp'=16] {'rep'}, dimensions={2}, use_global_device_ids=true | all-gather | bytes 473088 | tf_op jit(solution)/shard_map/all_gather | solution.py:26
  155.9 73.2 %all_gather.15 = f32[2,2,28672]{2,1,0:T(2,128)S(1)} all-gather(f32[2,2,896]{2,1,0:T(2,128)} %param.13), channel_id=1, replica_groups=mesh['rep'=32,'fsdp'=16] {'rep'}, dimensions={2}, use_global_device_ids=true | all-gather | bytes 473088 | tf_op jit(solution)/shard_map/all_gather | solution.py:27
  229.1 0.0 copy-done
  229.1 0.4 fusion.2
  229.5 79.8 %all-reduce.3.cloned.1.call-done = f32[2,2,28672]{2,1,0:T(2,128)} async-done(((f32[2,2,28672]{2,1,0:T(2,128)}), f32[2,2,28672]{2,1,0:T(2,128)}) %all-reduce.3.cloned.1.call-update) | async-done | bytes 458768 | tf_op jit(solution)/shard_map/psum | solution.py:23
  309.3 0.0 copy-done.1
  309.3 3.1 fusion.14
  312.4 0.6 constant_dynamic-slice_fusion.1
  313.0 1.4 multiply_add_fusion
  314.4 0.6 constant_dynamic-slice_fusion
  315.0 0.0 all-gather.2.cloned.1.call-done
  315.1 8.0 %fusion.8 = bf16[128,1024]{1,0:T(8,128)(2,1)} fusion(bf16[1,7168,1024]{2,1,0:T(8,128)(2,1)} %all-gather.2.cloned.1.call-done, bf16[128,7168]{1,0:T(8,128)(2,1)S(1)} %copy-done, f32[7168]{0:T(1024)S(1)} %mul.70, f32[128]{0:T(128)S(1)} %add_rsqrt_fusion), kind=kOutput, calls=%fused_computation.9 | convolution fusion | flops 1882849280 | bytes 16806400 | tf_op jit(solution)/shard_map/dot_general | solution.py:14
  (3 shorter events, 0.0 us)
Async XLA Ops:
  8.0 221.1 %copy-start = (bf16[128,7168]{1,0:T(8,128)(2,1)S(1)}, bf16[128,7168]{1,0:T(8,128)(2,1)}, u32[]{:S(2)}) copy-start(bf16[128,7168]{1,0:T(8,128)(2,1)} %param.17) | copy-start | bytes 5505028
  8.0 301.3 %copy-start.1 = (bf16[1,2,2,28672]{3,2,1,0:T(2,128)(2,1)S(1)}, bf16[1,2,2,28672]{3,2,1,0:T(2,128)(2,1)}, u32[]{:S(2)}) copy-start(bf16[1,2,2,28672]{3,2,1,0:T(2,128)(2,1)} %param.14) | copy-start | bytes 688132
  8.0 301.3 %all-reduce.3.cloned.1.call-start = ((), (), s32[]{:S(2)}) async-start(), calls=%async_computation.1 | async-start | bytes 917504 | tf_op jit(solution)/shard_map/psum | solution.py:23
  10.2 304.8 %all-gather.2.cloned.1.call-start = ((), (), s32[]{:S(2)}) async-start(), calls=%async_computation | async-start | bytes 15597568 | tf_op jit(solution)/shard_map/all_gather | solution.py:11
Sparse Core Ops, SparseCore 0:
  11.8 297.5 all-reduce.2
Sparse Core Ops, SparseCore 1:
  12.9 98.2 all-gather.1
where the time goes:
time: 335 us; the launch traced here: 330 us
  blocking collectives  213 us (64%)
  waiting for transfers between devices  80.3 us (24%)
  between operations  16.2 us (5%)
  other arithmetic  9.72 us (3%)
  matrix products  7.98 us (2%)
    all_gather x1, blocking collectives, outer_step(): lax.all_gather(outer_params, 'rep', axis=2, tiled=True)  84 us
    psum x1, waiting for transfers between devices, outer_step(): summed = lax.psum(term, 'rep')  79.8 us
    all_gather x1, blocking collectives, outer_step(): lax.all_gather(momentum, 'rep', axis=2, tiled=True)  73.2 us
    unnamed x1, blocking collectives  56.3 us
    dot_general x1, matrix products, inner_step(): total = jnp.dot(normed, weight_piece[0], preferred_element_type=jnp.float32)  7.98 us
  transfers between devices with their start and end apart: 2, of which 1 were waited for; matrix products, arithmetic and copies ran while one was open for 3% of the time, Pallas kernels for 0%

commit v1 on v0

v1 whole, which is shorter than its diff:
```python
import functools

import jax
import jax.numpy as jnp
from jax import lax
from jax.experimental import pallas as pl
from jax.experimental.pallas import tpu as pltpu
from jax.sharding import PartitionSpec as P

F32 = jnp.float32
BF16 = jnp.bfloat16
CHUNKS = 4
NX = 4


def remote(src, dst, send, recv, device):
    return pltpu.make_async_remote_copy(
        src_ref=src,
        dst_ref=dst,
        send_sem=send,
        recv_sem=recv,
        device_id=device,
        device_id_type=pl.DeviceIdType.MESH,
    )


def kernel(
    nz,
    scales,
    rates,
    slot,
    gain,
    tokens,
    weight,
    codes,
    params,
    moment,
    local,
    keyvals_out,
    outer_out,
    moment_out,
    blended_out,
    tok,
    xs,
    relay,
    wraw,
    wk,
    own,
    held,
    c2_send,
    c2_recv,
    c1_send,
    c1_recv,
    kv,
    cb,
    stage_far,
    stage_own,
    fs,
    fr,
    msg,
    rb,
    total,
    pm,
    res,
    rc,
    blocks,
    lp,
    bl,
    load_sem,
    tok_sem,
    wload_sem,
    out_sem,
    xs_send,
    xs_recv,
    rl_send,
    rl_recv,
    fw_send,
    wy_send,
    wy_recv,
    wc_send,
    wc_recv,
    wf_send,
    wf_recv,
    c2s,
    c2r,
    c1s,
    c1r,
    za_send,
    za_recv,
    zb_send,
    zb_recv,
    ph_send,
    ph_recv,
    fb_send,
    fb_recv,
    here,
):
    count = tokens.shape[0]
    width = tokens.shape[1] // 8
    cols = res.shape[3]
    wide = msg.shape[2]
    runs = [(g, g * wide, min(wide, cols - g * wide)) for g in range(4) if g * wide < cols]
    part = kv.shape[1] // CHUNKS
    shard = weight.shape[1]

    me_r = lax.axis_index("rep")
    me_f = lax.axis_index("fsdp")
    z, yh = lax.rem(me_r, nz), lax.div(me_r, nz)
    core, x, y = lax.rem(me_f, 2), lax.rem(lax.div(me_f, 2), NX), lax.div(me_f, 2 * NX)

    def on_x(step):
        return (me_r, y * (2 * NX) + lax.rem(x + step, NX) * 2 + core)

    right, left = on_x(1), on_x(NX - 1)
    across = (me_r, (1 - y) * (2 * NX) + x * 2 + core)
    twin = (me_r, me_f + 1 - 2 * core)
    far = (lax.rem(me_r + nz, 2 * nz), me_f)

    def on_z(k):
        return (yh * nz + lax.rem(z + k, nz), me_f)

    def signal(sem, device):
        pl.semaphore_signal(sem, inc=1, device_id=device, device_id_type=pl.DeviceIdType.MESH)

    barrier = pltpu.get_barrier_semaphore()
    neighbours = (right, left, across, twin, far, on_z(1), on_z(nz - 1))
    for device in neighbours:
        signal(barrier, device)

    def piece(owner, rel):
        h = y if rel == 0 else 1 - y
        start = pl.multiple_of((h * NX + owner) * width, 128)
        return tokens.at[:, pl.ds(start, width)]

    load_codes = pltpu.make_async_copy(codes.at[0], cb, load_sem.at[0])
    wloads = [
        pltpu.make_async_copy(
            weight.at[0, :, pl.ds(n * part, part)], wraw.at[n], wload_sem.at[n]
        )
        for n in range(CHUNKS)
    ]
    load_tok = [
        [
            pltpu.make_async_copy(
                piece(lax.rem(x + d, NX), rel),
                tok.at[rel, d] if d else xs.at[rel, 0],
                tok_sem.at[rel, d],
            )
            for d in range(NX)
        ]
        for rel in range(2)
    ]
    load_pm = [
        pltpu.make_async_copy(ref, pm.at[i], load_sem.at[4 + i])
        for i, ref in enumerate((params, moment))
    ]
    load_lp = pltpu.make_async_copy(local.at[0], lp, load_sem.at[6])
    load_tok[0][2].start()
    load_tok[1][2].start()
    load_codes.start()
    for copy in wloads:
        copy.start()
    for rel, d in ((0, 1), (0, 3), (1, 1), (1, 3), (0, 0), (1, 0)):
        load_tok[rel][d].start()
    for copy in load_pm + [load_lp]:
        copy.start()
    for stage in (stage_far, stage_own):
        stage[...] = jnp.zeros(stage.shape, F32)

    load_codes.wait()
    row_at = lax.broadcasted_iota(jnp.int32, (2, 1), 0)

    def terms(stage, half_y):
        for l in range(2):
            row_scale = jnp.where(row_at == 0, scales[0, l, 0], scales[0, l, 1])
            for to in range(nz):
                for g, start, size in runs:
                    at = pl.multiple_of((half_y * nz + to) * cols + start, 128)
                    row = g * 4 + l * 2
                    stage[to, row : row + 2, :size] = (
                        cb[l, :, pl.ds(at, size)].astype(F32) * row_scale
                    )

    terms(stage_far, 1 - yh)
    for to in range(nz):
        fs[to] = stage_far[to].astype(BF16)
    halves = remote(fs, fr, ph_send.at[0], ph_recv.at[0], far)

    pl.semaphore_wait(barrier, len(neighbours))
    halves.start()

    def tell(turn):
        if 2 ** (turn + 1) < nz:
            for step in (2**turn, nz - 2**turn):
                signal(here.at[turn], on_z(step))

    def learn(turn):
        if 2 ** (turn + 1) < nz:
            pl.semaphore_wait(here.at[turn], 2)

    tell(0)

    relays = [
        remote(tok.at[0, 2], relay.at[0], rl_send.at[0], rl_recv.at[0], right),
        remote(tok.at[1, 2], relay.at[1], rl_send.at[1], rl_recv.at[1], left),
    ]
    forwards = [
        remote(relay.at[0], xs.at[0, 2], fw_send.at[0], xs_recv.at[0, 2], right),
        remote(relay.at[1], xs.at[1, 2], fw_send.at[1], xs_recv.at[1, 2], left),
    ]
    directs = [
        [
            remote(
                tok.at[rel, d],
                xs.at[rel, NX - d],
                xs_send.at[rel, NX - d],
                xs_recv.at[rel, NX - d],
                device,
            )
            for d, device in ((1, right), (3, left))
        ]
        for rel in range(2)
    ]
    for rel in range(2):
        load_tok[rel][2].wait()
        relays[rel].start()
    at_row = lax.broadcasted_iota(jnp.int32, (shard, shard), 0)
    at_col = lax.broadcasted_iota(jnp.int32, (shard, shard), 1)
    gain_col = jnp.sum(
        jnp.where(at_row == at_col, gain[...].astype(F32), 0.0), axis=1, keepdims=True
    )
    w_across = [
        remote(wk.at[n, 0, core], wk.at[n, 1, core], wy_send.at[n], wy_recv.at[n], across)
        for n in range(CHUNKS)
    ]
    w_twin = [
        remote(wk.at[n, 0, core], wk.at[n, 0, core], wc_send.at[n], wc_recv.at[n], twin)
        for n in range(CHUNKS)
    ]
    w_forward = [
        remote(wk.at[n, 1, core], wk.at[n, 1, core], wf_send.at[n], wf_recv.at[n], twin)
        for n in range(CHUNKS)
    ]

    def scale_chunk(n):
        wloads[n].wait()
        wk[n, 0, core] = (wraw[n].astype(F32) * gain_col).astype(BF16)
        w_across[n].start()
        w_twin[n].start()

    def send_direct(rel):
        for i, d in enumerate((1, 3)):
            load_tok[rel][d].wait()
            directs[rel][i].start()

    scale_chunk(0)
    send_direct(0)
    learn(0)
    tell(1)
    scale_chunk(1)
    terms(stage_own, yh)
    learn(1)
    tell(2)

    halves.wait_recv()
    for to in range(nz):
        stage_own[to] = stage_own[to] + fr[to].astype(F32)
        msg[to] = stage_own[to].astype(BF16)
    learn(2)

    def offset(i):
        return nz // 2 + (1 - 2 * lax.rem(i, 2)) * lax.div(i + 1, 2)

    def z_terms(k):
        return remote(msg.at[lax.rem(z + k, nz)], rb.at[k], za_send.at[k], za_recv.at[k], on_z(k))

    def send_terms(i, carry):
        z_terms(offset(i)).start()
        return carry

    lax.fori_loop(0, nz - 1, send_terms, 0)
    for rel in range(2):
        relays[rel].wait_recv()
        forwards[rel].start()
    send_direct(1)
    directs = directs[0] + directs[1]
    for n in range(2, CHUNKS):
        scale_chunk(n)

    squares = jnp.zeros((count, 1), F32)
    for rel in range(2):
        load_tok[rel][0].wait()
        for d in range(NX):
            block = (tok[rel, d] if d else xs[rel, 0]).astype(F32)
            squares += jnp.sum(block * block, axis=1, keepdims=True)
    inverse = lax.rsqrt(squares / tokens.shape[1] + 1e-05)

    def pass_on(n):
        w_across[n].wait_recv()
        w_forward[n].start()

    pass_on(0)

    def add_terms(k, total):
        z_terms(k).wait_recv()
        return total + rb[k].astype(F32)

    total[...] = lax.fori_loop(1, nz, add_terms, stage_own[z]) / (2 * nz)
    for copy in load_pm:
        copy.wait()
    rate = rates[slot[0]]
    for l in range(2):
        for g, start, size in runs:
            row = g * 4 + l * 2
            at = slice(start, start + size)
            mean_delta = total[row : row + 2, :size]
            new_moment = 0.9 * pm[1, l, :, at] + mean_delta
            new_outer = pm[0, l, :, at] - rate * (mean_delta + 0.9 * new_moment)
            res[0, l, :, at] = new_outer
            res[1, l, :, at] = new_moment
            total[row : row + 2, :size] = new_outer
    rc[yh, z] = total[...].astype(BF16)

    def z_outer(k, source):
        block = rc.at[yh, source]
        return remote(block, block, zb_send.at[k], zb_recv.at[source], on_z(k))

    def send_outer(i, carry):
        z_outer(offset(i), z).start()
        return carry

    lax.fori_loop(0, nz - 1, send_outer, 0)
    outs = [
        pltpu.make_async_copy(res.at[i], ref, out_sem.at[i])
        for i, ref in enumerate((outer_out, moment_out))
    ]
    for copy in outs:
        copy.start()

    pass_on(1)
    pass_on(2)
    for copy in directs + forwards:
        copy.wait_recv()

    sides = (right, left)
    c2 = [
        remote(c2_send.at[n], c2_recv.at[n], c2s.at[n], c2r.at[n], sides[n % 2])
        for n in range(CHUNKS)
    ]
    c1 = [
        [
            remote(c1_send.at[n, s], c1_recv.at[n, s], c1s.at[n, s], c1r.at[n, s], sides[s])
            for s in range(2)
        ]
        for n in range(CHUNKS)
    ]
    rows_of = {0: 1, 1: 3}

    def multiply(n):
        w_twin[n].wait_recv()
        w_forward[n].wait_recv()
        whole = sum(
            jnp.dot(
                xs[rel].reshape(NX * count, width),
                wk[n, rel].reshape(width, part),
                preferred_element_type=F32,
            )
            for rel in range(2)
        )

        def rows(d):
            return whole[d * count : (d + 1) * count]

        via, other = n % 2, 1 - n % 2
        c2_send[n] = rows(2).astype(BF16)
        c2[n].start()
        c1_send[n, other] = rows(rows_of[other]).astype(BF16)
        c1[n][other].start()
        held[n] = rows(rows_of[via])
        own[n] = rows(0)

    def combine(n):
        via = n % 2
        c2[n].wait_recv()
        c1_send[n, via] = (held[n] + c2_recv[n].astype(F32)).astype(BF16)
        c1[n][via].start()

    def finish(n):
        for s in range(2):
            c1[n][s].wait_recv()
        at = n * part
        whole = own[n] + c1_recv[n, 0].astype(F32) + c1_recv[n, 1].astype(F32)
        kv[:, at : at + part] = (whole * inverse).astype(BF16)

    multiply(0)
    multiply(1)
    combine(0)
    multiply(2)
    combine(1)
    pass_on(3)
    combine(2)
    multiply(3)

    def quarter(turn):
        return lax.rem(lax.div(z, 4) + turn, nz // 4)

    def hand_over(turn):
        block = rc.at[yh, pl.ds(quarter(turn) * 4, 4)]
        return remote(block, block, fb_send.at[turn], fb_recv.at[turn], far)

    for turn in range(nz // 4):
        for i in range(4):
            source = quarter(turn) * 4 + i

            @pl.when(source != z)
            def _():
                z_outer(0, source).wait_recv()

        hand_over(turn).start()
    combine(3)

    load_lp.wait()

    def blend(half_y, turn):
        for i in range(4):
            source = quarter(turn) * 4 + i
            blocks[i] = rc[half_y, source].astype(F32)
            for l in range(2):
                for g, start, size in runs:
                    row = g * 4 + l * 2
                    at = pl.ds(pl.multiple_of((half_y * nz + source) * cols + start, 128), size)
                    mine = lp[l, :, at].astype(F32)
                    new = blocks[i, row : row + 2, :size]
                    bl[l, :, at] = (0.5 * mine + 0.5 * new).astype(BF16)

    for turn in range(nz // 4):
        blend(yh, turn)
    for n in range(CHUNKS):
        finish(n)
    out_kv = pltpu.make_async_copy(kv, keyvals_out, out_sem.at[3])
    out_kv.start()
    for turn in range(nz // 4):
        hand_over(turn).wait_recv()
        blend(1 - yh, turn)
    out_blend = pltpu.make_async_copy(bl, blended_out.at[0], out_sem.at[2])
    out_blend.start()


    for copy in relays + directs + forwards + w_across + w_twin + w_forward + [halves] + c2:
        copy.wait_send()
    for turn in range(nz // 4):
        hand_over(turn).wait_send()
    for pair in c1:
        for copy in pair:
            copy.wait_send()

    def drain(k, carry):
        z_terms(k).wait_send()
        z_outer(k, z).wait_send()
        return carry

    lax.fori_loop(1, nz, drain, 0)
    for copy in outs + [out_blend, out_kv]:
        copy.wait()


def place(*refs):
    count = (len(refs) - 2) // 3
    sources, results, held = refs[:count], refs[count : 2 * count], refs[2 * count : 3 * count]
    into, out = refs[3 * count :]
    loads = [pltpu.make_async_copy(sources[i], held[i], into.at[i]) for i in range(count)]
    stores = [pltpu.make_async_copy(held[i], results[i], out.at[i]) for i in range(count)]
    for copy in loads:
        copy.start()
    for load, store in zip(loads, stores):
        load.wait()
        store.start()
    for copy in stores:
        copy.wait()


def shards(
    codes, scales, outer_params, momentum, local_params, rates, slot, tokens, gain, kv_weight
):
    nz = lax.axis_size("rep") // 2
    count, depth = tokens.shape
    width = depth // 8
    out_cols = kv_weight.shape[2]
    part = out_cols // CHUNKS
    shard = kv_weight.shape[1]
    full = codes.shape[3]
    cols = outer_params.shape[2]
    wide = (cols // 128 + 3) // 4 * 128
    dma = pltpu.SemaphoreType.DMA
    smem = pl.BlockSpec(memory_space=pltpu.SMEM)
    hbm = pl.BlockSpec(memory_space=pl.ANY)
    scratch = [
        pltpu.VMEM((2, NX, count, width), BF16),
        pltpu.VMEM((2, NX, count, width), BF16),
        pltpu.VMEM((2, count, width), BF16),
        pltpu.VMEM((CHUNKS, shard, part), BF16),
        pltpu.VMEM((CHUNKS, 2, 2, shard, part), BF16),
        pltpu.VMEM((CHUNKS, count, part), F32),
        pltpu.VMEM((CHUNKS, count, part), F32),
        pltpu.VMEM((CHUNKS, count, part), BF16),
        pltpu.VMEM((CHUNKS, count, part), BF16),
        pltpu.VMEM((CHUNKS, 2, count, part), BF16),
        pltpu.VMEM((CHUNKS, 2, count, part), BF16),
        pltpu.VMEM((count, out_cols), BF16),
        pltpu.VMEM((2, 2, full), jnp.int32),
        pltpu.VMEM((nz, 16, wide), F32),
        pltpu.VMEM((nz, 16, wide), F32),
        pltpu.VMEM((nz, 16, wide), BF16),
        pltpu.VMEM((nz, 16, wide), BF16),
        pltpu.VMEM((nz, 16, wide), BF16),
        pltpu.VMEM((nz, 16, wide), BF16),
        pltpu.VMEM((16, wide), F32),
        pltpu.VMEM((2, 2, 2, cols), F32),
        pltpu.VMEM((2, 2, 2, cols), F32),
        pltpu.VMEM((2, nz, 16, wide), BF16),
        pltpu.VMEM((4, 16, wide), F32),
        pltpu.VMEM((2, 2, full), BF16),
        pltpu.VMEM((2, 2, full), BF16),
        dma((7,)),
        dma((2, NX)),
        dma((CHUNKS,)),
        dma((4,)),
        dma((2, NX)),
        dma((2, NX)),
        dma((2,)),
        dma((2,)),
        dma((2,)),
        dma((CHUNKS,)),
        dma((CHUNKS,)),
        dma((CHUNKS,)),
        dma((CHUNKS,)),
        dma((CHUNKS,)),
        dma((CHUNKS,)),
        dma((CHUNKS,)),
        dma((CHUNKS,)),
        dma((CHUNKS, 2)),
        dma((CHUNKS, 2)),
        dma((nz,)),
        dma((nz,)),
        dma((nz,)),
        dma((nz,)),
        dma((1,)),
        dma((1,)),
        dma((4,)),
        dma((4,)),
        pltpu.SemaphoreType.REGULAR((4,)),
    ]
    results = pl.pallas_call(
        functools.partial(kernel, nz),
        out_shape=(
            jax.ShapeDtypeStruct((count, out_cols), BF16),
            jax.ShapeDtypeStruct(outer_params.shape, F32),
            jax.ShapeDtypeStruct(momentum.shape, F32),
            jax.ShapeDtypeStruct(local_params.shape, BF16),
        ),
        in_specs=[smem, smem, smem, pl.BlockSpec(memory_space=pltpu.VMEM)] + [hbm] * 6,
        out_specs=(hbm,) * 4,
        scratch_shapes=scratch,
        compiler_params=pltpu.CompilerParams(
            collective_id=0, has_side_effects=True, vmem_limit_bytes=60 * 2**20
        ),
        cost_estimate=pl.CostEstimate(
            flops=2 * count * depth * out_cols, bytes_accessed=8 * 2**20, transcendentals=count
        ),
    )(scales, rates, slot, gain, tokens, kv_weight, codes, outer_params, momentum, local_params)
    return pl.pallas_call(
        place,
        out_shape=tuple(jax.ShapeDtypeStruct(r.shape, r.dtype) for r in results),
        in_specs=[hbm] * len(results),
        out_specs=(hbm,) * len(results),
        scratch_shapes=[pltpu.VMEM(r.shape, r.dtype) for r in results]
        + [dma((len(results),))] * 2,
        compiler_params=pltpu.CompilerParams(vmem_limit_bytes=60 * 2**20),
    )(*results)


def solution(mesh):
    return jax.shard_map(
        shards,
        mesh=mesh,
        in_specs=(
            P("rep", None, "fsdp", None),
            P("rep", None, "fsdp"),
            P(None, "fsdp", "rep"),
            P(None, "fsdp", "rep"),
            P("rep", None, "fsdp", None),
            P(),
            P(),
            P(("rep", "fsdp"), None),
            P("rep", "fsdp"),
            P("rep", "fsdp", None),
        ),
        out_specs=(
            P(("rep", "fsdp"), None),
            P(None, "fsdp", "rep"),
            P(None, "fsdp", "rep"),
            P("rep", None, "fsdp", None),
        ),
        check_vma=False,
    )
```

time: 335 us -> 57.1 us (0.17); the launches traced: 330 us -> 57 us
  blocking collectives: 213 us -> 0 us
  waiting for transfers between devices: 80.3 us -> 0 us
  Pallas kernels: 0 us -> 56.3 us
  between operations: 16.2 us -> 0.64 us
  other arithmetic: 9.72 us -> 0 us
  matrix products: 7.98 us -> 0 us
    all_gather x2 -> x0, blocking collectives: 157 us -> none  [the longest x1 84 us: outer_step(): lax.all_gather(outer_params, 'rep', axis=2, tiled=True)]
    psum x1 -> x0, waiting for transfers between devices: 79.8 us -> none  [outer_step(): summed = lax.psum(term, 'rep')]
    pallas_call x0 -> x2, Pallas kernels: none -> 56.3 us  [the longest x1 54.5 us: shards(): pl.pallas_call(functools.partial(kernel, nz), out_shape=(jax.ShapeDtypeSt...]
    unnamed x1 -> x0, blocking collectives: 56.3 us -> none
    dot_general x1 -> x0, matrix products: 7.98 us -> none  [inner_step(): total = jnp.dot(normed, weight_piece[0], preferred_element_type=jnp.float32)]
  transfers between devices with their start and end apart: 2 -> 0, of which waited for: 1 -> 0; matrix products, arithmetic and copies ran while one was open for 3% -> 0% of each run, Pallas kernels for 0% -> 0%
where the time goes in v1:
time: 57.1 us; the launch traced here: 57 us
  Pallas kernels  56.3 us (99%)
  between operations  0.64 us (1%)
    pallas_call x1, Pallas kernels, shards(): pl.pallas_call(functools.partial(kernel, nz), out_shape=(jax.ShapeDtypeSt...  54.5 us
    pallas_call x1, Pallas kernels, shards(): pl.pallas_call(place, out_shape=tuple((jax.ShapeDtypeStruct(r.shape, r.dt...  1.81 us

profile of v1, /device:TPU:24, one launch (start us, length us, event | category | flops | bytes accessed | tf_op | source)
XLA Modules:
  0.0 57.0 jit_solution(9069256756897293619)
XLA Ops:
  0.6 54.5 %shard_map.129 = (bf16[128,1024]{1,0:T(8,128)(2,1)}, f32[2,2,896]{2,1,0:T(2,128)}, f32[2,2,896]{2,1,0:T(2,128)}, bf16[1,2,2,28672]{3,2,1,0:T(2,128)(2,1)}) custom-call(f32[1,2,2]{2,1,0:T(2,128)} %scales.1, f32[32]{0:T(128)} %rates.1, s32[32]{0:T(128)} %slot.1, bf16[1,448]{1,0:T(2,128)(2,1)} %gain.1, bf16[128,7168]{1,0:T(8,128)(2,1)} %tokens.1, ...), custom_call_target="tpu_custom_call" | custom-call | flops 1879048192 | bytes 8388608 | tf_op jit(solution)/shard_map/pallas_call | solution.py:553
  55.2 1.8 %shard_map.130 = (bf16[128,1024]{1,0:T(8,128)(2,1)}, f32[2,2,896]{2,1,0:T(2,128)}, f32[2,2,896]{2,1,0:T(2,128)}, bf16[1,2,2,28672]{3,2,1,0:T(2,128)(2,1)}) custom-call(bf16[128,1024]{1,0:T(8,128)(2,1)} %get-tuple-element.8.refs_0_, f32[2,2,896]{2,1,0:T(2,128)} %get-tuple-element.9.refs_1_, f32[2,2,896]{2,1,0:T(2,128)} %get-tuple-element.10.refs_2_, ...), custom_call_target="tpu_custom_call" | custom-call | tf_op jit(solution)/shard_map/pallas_call | solution.py:571

commit v2 on v1

--- a/solution.py
+++ b/solution.py
@@ -259,6 +259,8 @@
     tell(1)
     scale_chunk(1)
     terms(stage_own, yh)
+    scale_chunk(2)
+    scale_chunk(3)
     learn(1)
     tell(2)
 
@@ -284,8 +286,6 @@
         forwards[rel].start()
     send_direct(1)
     directs = directs[0] + directs[1]
-    for n in range(2, CHUNKS):
-        scale_chunk(n)
 
     squares = jnp.zeros((count, 1), F32)
     for rel in range(2):
@@ -433,8 +433,15 @@
                     new = blocks[i, row : row + 2, :size]
                     bl[l, :, at] = (0.5 * mine + 0.5 * new).astype(BF16)
 
+    def write_half(half_y, sem):
+        at = pl.ds(pl.multiple_of(half_y * nz * cols, 128), nz * cols)
+        copy = pltpu.make_async_copy(bl.at[:, :, at], blended_out.at[0, :, :, at], sem)
+        copy.start()
+        return copy
+
     for turn in range(nz // 4):
         blend(yh, turn)
+    out_near = write_half(yh, out_sem.at[2])
     for n in range(CHUNKS):
         finish(n)
     out_kv = pltpu.make_async_copy(kv, keyvals_out, out_sem.at[3])
@@ -442,8 +449,7 @@
     for turn in range(nz // 4):
         hand_over(turn).wait_recv()
         blend(1 - yh, turn)
-    out_blend = pltpu.make_async_copy(bl, blended_out.at[0], out_sem.at[2])
-    out_blend.start()
+    out_far = write_half(1 - yh, out_sem.at[4])
 
 
     for copy in relays + directs + forwards + w_across + w_twin + w_forward + [halves] + c2:
@@ -460,7 +466,7 @@
         return carry
 
     lax.fori_loop(1, nz, drain, 0)
-    for copy in outs + [out_blend, out_kv]:
+    for copy in outs + [out_near, out_far, out_kv]:
         copy.wait()
 
 
@@ -524,7 +530,7 @@
         dma((7,)),
         dma((2, NX)),
         dma((CHUNKS,)),
-        dma((4,)),
+        dma((5,)),
         dma((2, NX)),
         dma((2, NX)),
         dma((2,)),

time: 57.1 us -> 57.1 us (level)
  no operation moved by 1% of the time
where the time goes in v2:
time: 57.1 us; the launch traced here: 56.9 us
  Pallas kernels  56.3 us (99%)
  between operations  0.64 us (1%)
    pallas_call x1, Pallas kernels, shards(): pl.pallas_call(functools.partial(kernel, nz), out_shape=(jax.ShapeDtypeSt...  54.5 us
    pallas_call x1, Pallas kernels, shards(): pl.pallas_call(place, out_shape=tuple((jax.ShapeDtypeStruct(r.shape, r.dt...  1.81 us

profile of v2, /device:TPU:24, one launch (start us, length us, event | category | flops | bytes accessed | tf_op | source)
XLA Modules:
  0.0 56.9 jit_solution(11401722516049477404)
XLA Ops:
  0.6 54.5 %shard_map.129 = (bf16[128,1024]{1,0:T(8,128)(2,1)}, f32[2,2,896]{2,1,0:T(2,128)}, f32[2,2,896]{2,1,0:T(2,128)}, bf16[1,2,2,28672]{3,2,1,0:T(2,128)(2,1)}) custom-call(f32[1,2,2]{2,1,0:T(2,128)} %scales.1, f32[32]{0:T(128)} %rates.1, s32[32]{0:T(128)} %slot.1, bf16[1,448]{1,0:T(2,128)(2,1)} %gain.1, bf16[128,7168]{1,0:T(8,128)(2,1)} %tokens.1, ...), custom_call_target="tpu_custom_call" | custom-call | flops 1879048192 | bytes 8388608 | tf_op jit(solution)/shard_map/pallas_call | solution.py:559
  55.1 1.8 %shard_map.130 = (bf16[128,1024]{1,0:T(8,128)(2,1)}, f32[2,2,896]{2,1,0:T(2,128)}, f32[2,2,896]{2,1,0:T(2,128)}, bf16[1,2,2,28672]{3,2,1,0:T(2,128)(2,1)}) custom-call(bf16[128,1024]{1,0:T(8,128)(2,1)} %get-tuple-element.8.refs_0_, f32[2,2,896]{2,1,0:T(2,128)} %get-tuple-element.9.refs_1_, f32[2,2,896]{2,1,0:T(2,128)} %get-tuple-element.10.refs_2_, ...), custom_call_target="tpu_custom_call" | custom-call | tf_op jit(solution)/shard_map/pallas_call | solution.py:577

commit v3 on v2

--- a/solution.py
+++ b/solution.py
@@ -254,15 +254,13 @@
             directs[rel][i].start()
 
     scale_chunk(0)
-    send_direct(0)
     learn(0)
     tell(1)
+    send_direct(0)
     scale_chunk(1)
-    terms(stage_own, yh)
-    scale_chunk(2)
-    scale_chunk(3)
     learn(1)
     tell(2)
+    terms(stage_own, yh)
 
     halves.wait_recv()
     for to in range(nz):
@@ -281,6 +279,8 @@
         return carry
 
     lax.fori_loop(0, nz - 1, send_terms, 0)
+    scale_chunk(2)
+    scale_chunk(3)
     for rel in range(2):
         relays[rel].wait_recv()
         forwards[rel].start()
@@ -298,8 +298,6 @@
     def pass_on(n):
         w_across[n].wait_recv()
         w_forward[n].start()
-
-    pass_on(0)
 
     def add_terms(k, total):
         z_terms(k).wait_recv()
@@ -337,6 +335,7 @@
     for copy in outs:
         copy.start()
 
+    pass_on(0)
     pass_on(1)
     pass_on(2)
     for copy in directs + forwards:

time: 57.1 us -> 57.1 us (level)
  no operation moved by 1% of the time
where the time goes in v3:
time: 57.1 us; the launch traced here: 56.9 us
  Pallas kernels  56.3 us (99%)
  between operations  0.64 us (1%)
    pallas_call x1, Pallas kernels, shards(): pl.pallas_call(functools.partial(kernel, nz), out_shape=(jax.ShapeDtypeSt...  54.5 us
    pallas_call x1, Pallas kernels, shards(): pl.pallas_call(place, out_shape=tuple((jax.ShapeDtypeStruct(r.shape, r.dt...  1.81 us

profile of v3, /device:TPU:24, one launch (start us, length us, event | category | flops | bytes accessed | tf_op | source)
XLA Modules:
  0.0 56.9 jit_solution(15144995161516689694)
XLA Ops:
  0.6 54.5 %shard_map.129 = (bf16[128,1024]{1,0:T(8,128)(2,1)}, f32[2,2,896]{2,1,0:T(2,128)}, f32[2,2,896]{2,1,0:T(2,128)}, bf16[1,2,2,28672]{3,2,1,0:T(2,128)(2,1)}) custom-call(f32[1,2,2]{2,1,0:T(2,128)} %scales.1, f32[32]{0:T(128)} %rates.1, s32[32]{0:T(128)} %slot.1, bf16[1,448]{1,0:T(2,128)(2,1)} %gain.1, bf16[128,7168]{1,0:T(8,128)(2,1)} %tokens.1, ...), custom_call_target="tpu_custom_call" | custom-call | flops 1879048192 | bytes 8388608 | tf_op jit(solution)/shard_map/pallas_call | solution.py:558
  55.1 1.8 %shard_map.130 = (bf16[128,1024]{1,0:T(8,128)(2,1)}, f32[2,2,896]{2,1,0:T(2,128)}, f32[2,2,896]{2,1,0:T(2,128)}, bf16[1,2,2,28672]{3,2,1,0:T(2,128)(2,1)}) custom-call(bf16[128,1024]{1,0:T(8,128)(2,1)} %get-tuple-element.8.refs_0_, f32[2,2,896]{2,1,0:T(2,128)} %get-tuple-element.9.refs_1_, f32[2,2,896]{2,1,0:T(2,128)} %get-tuple-element.10.refs_2_, ...), custom_call_target="tpu_custom_call" | custom-call | tf_op jit(solution)/shard_map/pallas_call | solution.py:576

commit v4 on v3

--- a/solution.py
+++ b/solution.py
@@ -396,9 +396,7 @@
     combine(0)
     multiply(2)
     combine(1)
-    pass_on(3)
     combine(2)
-    multiply(3)
 
     def quarter(turn):
         return lax.rem(lax.div(z, 4) + turn, nz // 4)
@@ -416,6 +414,8 @@
                 z_outer(0, source).wait_recv()
 
         hand_over(turn).start()
+    pass_on(3)
+    multiply(3)
     combine(3)
 
     load_lp.wait()
@@ -470,17 +470,12 @@
 
 
 def place(*refs):
-    count = (len(refs) - 2) // 3
-    sources, results, held = refs[:count], refs[count : 2 * count], refs[2 * count : 3 * count]
-    into, out = refs[3 * count :]
-    loads = [pltpu.make_async_copy(sources[i], held[i], into.at[i]) for i in range(count)]
-    stores = [pltpu.make_async_copy(held[i], results[i], out.at[i]) for i in range(count)]
-    for copy in loads:
+    count = len(refs) // 2
+    sems = refs[-1]
+    copies = [pltpu.make_async_copy(refs[i], refs[count + i], sems.at[i]) for i in range(count)]
+    for copy in copies:
         copy.start()
-    for load, store in zip(loads, stores):
-        load.wait()
-        store.start()
-    for copy in stores:
+    for copy in copies:
         copy.wait()
 
 
@@ -558,13 +553,13 @@
     results = pl.pallas_call(
         functools.partial(kernel, nz),
         out_shape=(
-            jax.ShapeDtypeStruct((count, out_cols), BF16),
-            jax.ShapeDtypeStruct(outer_params.shape, F32),
-            jax.ShapeDtypeStruct(momentum.shape, F32),
-            jax.ShapeDtypeStruct(local_params.shape, BF16),
+            pltpu.VMEM((count, out_cols), BF16),
+            pltpu.VMEM(outer_params.shape, F32),
+            pltpu.VMEM(momentum.shape, F32),
+            pltpu.VMEM(local_params.shape, BF16),
         ),
         in_specs=[smem, smem, smem, pl.BlockSpec(memory_space=pltpu.VMEM)] + [hbm] * 6,
-        out_specs=(hbm,) * 4,
+        out_specs=(pl.BlockSpec(memory_space=pltpu.VMEM),) * 4,
         scratch_shapes=scratch,
         compiler_params=pltpu.CompilerParams(
             collective_id=0, has_side_effects=True, vmem_limit_bytes=60 * 2**20
@@ -576,11 +571,10 @@
     return pl.pallas_call(
         place,
         out_shape=tuple(jax.ShapeDtypeStruct(r.shape, r.dtype) for r in results),
-        in_specs=[hbm] * len(results),
+        in_specs=[pl.BlockSpec(memory_space=pltpu.VMEM)] * len(results),
         out_specs=(hbm,) * len(results),
-        scratch_shapes=[pltpu.VMEM(r.shape, r.dtype) for r in results]
-        + [dma((len(results),))] * 2,
-        compiler_params=pltpu.CompilerParams(vmem_limit_bytes=60 * 2**20),
+        scratch_shapes=[dma((len(results),))],
+        compiler_params=pltpu.CompilerParams(vmem_limit_bytes=8 * 2**20),
     )(*results)
 
 

time: 57.1 us -> 56.7 us (level); the launches traced: 56.9 us -> 55.6 us
  Pallas kernels: 56.3 us -> 55 us
    pallas_call x1, Pallas kernels: 1.81 us -> 0.82 us  [shards(): pl.pallas_call(place, out_shape=tuple((jax.ShapeDtypeStruct(r.shape, r.dt...]
where the time goes in v4:
time: 56.7 us; the launch traced here: 55.6 us
  Pallas kernels  55 us (97%)
  between operations  0.64 us (1%)
    pallas_call x1, Pallas kernels, shards(): pl.pallas_call(functools.partial(kernel, nz), out_shape=(pltpu.VMEM((coun...  54.2 us

profile of v4, /device:TPU:24, one launch (start us, length us, event | category | flops | bytes accessed | tf_op | source)
XLA Modules:
  0.0 55.6 jit_solution(18378911196719744268)
XLA Ops:
  0.6 54.2 %shard_map.129 = (bf16[128,1024]{1,0:T(8,128)(2,1)S(1)}, f32[2,2,896]{2,1,0:T(2,128)S(1)}, f32[2,2,896]{2,1,0:T(2,128)S(1)}, bf16[1,2,2,28672]{3,2,1,0:T(2,128)(2,1)S(1)}) custom-call(f32[1,2,2]{2,1,0:T(2,128)} %scales.1, f32[32]{0:T(128)} %rates.1, s32[32]{0:T(128)} %slot.1, bf16[1,448]{1,0:T(2,128)(2,1)} %gain.1, bf16[128,7168]{1,0:T(8,128)(2,1)} %tokens.1, ...), custom_call_target="tpu_custom_call" | custom-call | flops 1879048192 | bytes 8388608 | tf_op jit(solution)/shard_map/pallas_call | solution.py:553
  54.8 0.8 %shard_map.130 = (bf16[128,1024]{1,0:T(8,128)(2,1)}, f32[2,2,896]{2,1,0:T(2,128)}, f32[2,2,896]{2,1,0:T(2,128)}, bf16[1,2,2,28672]{3,2,1,0:T(2,128)(2,1)}) custom-call(bf16[128,1024]{1,0:T(8,128)(2,1)S(1)} %get-tuple-element.8.refs_0_, f32[2,2,896]{2,1,0:T(2,128)S(1)} %get-tuple-element.9.refs_1_, f32[2,2,896]{2,1,0:T(2,128)S(1)} %get-tuple-element.10.refs_2_, ...), custom_call_target="tpu_custom_call" | custom-call | tf_op jit(solution)/shard_map/pallas_call | solution.py:571

commit v5 on v4

--- a/solution.py
+++ b/solution.py
@@ -396,6 +396,7 @@
     combine(0)
     multiply(2)
     combine(1)
+    pass_on(3)
     combine(2)
 
     def quarter(turn):
@@ -414,7 +415,6 @@
                 z_outer(0, source).wait_recv()
 
         hand_over(turn).start()
-    pass_on(3)
     multiply(3)
     combine(3)
 

time: 56.7 us -> 55.7 us (0.982); the launches traced: 55.6 us -> 55.5 us
  no operation moved by 1% of the time
where the time goes in v5:
time: 55.7 us; the launch traced here: 55.5 us
  Pallas kernels  54.9 us (99%)
  between operations  0.64 us (1%)
    pallas_call x1, Pallas kernels, shards(): pl.pallas_call(functools.partial(kernel, nz), out_shape=(pltpu.VMEM((coun...  54.1 us

profile of v5, /device:TPU:24, one launch (start us, length us, event | category | flops | bytes accessed | tf_op | source)
XLA Modules:
  0.0 55.5 jit_solution(17071759049238864639)
XLA Ops:
  0.6 54.1 %shard_map.129 = (bf16[128,1024]{1,0:T(8,128)(2,1)S(1)}, f32[2,2,896]{2,1,0:T(2,128)S(1)}, f32[2,2,896]{2,1,0:T(2,128)S(1)}, bf16[1,2,2,28672]{3,2,1,0:T(2,128)(2,1)S(1)}) custom-call(f32[1,2,2]{2,1,0:T(2,128)} %scales.1, f32[32]{0:T(128)} %rates.1, s32[32]{0:T(128)} %slot.1, bf16[1,448]{1,0:T(2,128)(2,1)} %gain.1, bf16[128,7168]{1,0:T(8,128)(2,1)} %tokens.1, ...), custom_call_target="tpu_custom_call" | custom-call | flops 1879048192 | bytes 8388608 | tf_op jit(solution)/shard_map/pallas_call | solution.py:553
  54.7 0.8 %shard_map.130 = (bf16[128,1024]{1,0:T(8,128)(2,1)}, f32[2,2,896]{2,1,0:T(2,128)}, f32[2,2,896]{2,1,0:T(2,128)}, bf16[1,2,2,28672]{3,2,1,0:T(2,128)(2,1)}) custom-call(bf16[128,1024]{1,0:T(8,128)(2,1)S(1)} %get-tuple-element.8.refs_0_, f32[2,2,896]{2,1,0:T(2,128)S(1)} %get-tuple-element.9.refs_1_, f32[2,2,896]{2,1,0:T(2,128)S(1)} %get-tuple-element.10.refs_2_, ...), custom_call_target="tpu_custom_call" | custom-call | tf_op jit(solution)/shard_map/pallas_call | solution.py:571
